TPU v7x, 256 devices: a whole 4x4x8 slice. The times are simulated.
256 devices in a mesh: row: 32 (over x, y, core), col: 8 (over z).
Axes of the slice: x: 4, y: 4, z: 8, core: 2. Of those that a mesh axis runs over, the one named last changes fastest.
Arguments:
- in_map: bfloat16 [512, 256, 256], P('row', 'col'), may hold values from -6 to 6
- tile_w: bfloat16 [3, 3, 256, 256], replicated, may hold values from -0.125 to 0.125
- head_w1: bfloat16 [3, 3, 256, 256], replicated, may hold values from -0.125 to 0.125
- head_w2: bfloat16 [3, 3, 256, 256], replicated, may hold values from -0.125 to 0.125
- box_row: int32 [512, 8], P('row', 'col'), may hold values from 0 to 2
- box_col: int32 [512, 8], P('row', 'col'), may hold values from 0 to 18
- box_target: int32 [512, 8], P('row', 'col'), may hold values from -1 to 31, as said below
- head_cot: bfloat16 [128, 8, 14, 14, 256], P('row', 'col'), may hold values from -6 to 6
Outputs:
- grad_map: bfloat16 [512, 256, 256], P('row', 'col')
- grad_w1: float32 [3, 3, 256, 256], replicated
- grad_w2: float32 [3, 3, 256, 256], replicated
Inputs may be any that keep to these rules, and one draw needn't show every extreme that they name: `box_target`: within each row r of tiles, every head slot d * 4 + h (d below 8, h below 4) is named by exactly one tile slot, and empty slots hold -1. A tile names at most 2 head slots of one device, so it holds at most 16 boxes; in every row of tiles one tile holds 16 boxes, 2 for each device of the row.
All inputs are finite; a program needn't handle non-finite values.
Results may differ from a plain program's by a relative error of at most 0.012.
Values may be sent and summed in bfloat16 or wider, within the bound.
A program may use at most 64 MiB of HBM per device.

v0:
```python
import math
import jax
import jax.numpy as jnp
from jax import lax
from jax.sharding import PartitionSpec as P

LAYOUT = ("NHWC", "HWIO", "NHWC")


def padded_2(shard, sides, width):
    for axis, dim in sides:
        size, length = (lax.axis_size(axis), shard.shape[dim])
        up = [(i, (i + 1) % size) for i in range(size - 1)]
        down = [(j, i) for i, j in up]
        last = lax.slice_in_dim(shard, length - width, length, axis=dim)
        leading = lax.slice_in_dim(shard, 0, width, axis=dim)
        before = lax.ppermute(last, axis, up)
        after = lax.ppermute(leading, axis, down)
        shard = jnp.concatenate([before, shard, after], axis=dim)
    return shard


def conv_pad(inputs, kernel, margin):
    return lax.conv_general_dilated(
        inputs,
        kernel,
        (1, 1),
        ((margin, margin), (margin, margin)),
        dimension_numbers=LAYOUT,
        preferred_element_type=jnp.float32,
    )


def flip_weights(kernel):
    return jnp.transpose(jnp.flip(kernel, (0, 1)), (0, 1, 3, 2))


def silu_slope(values):
    sigma = jax.nn.sigmoid(values)
    return sigma * (1.0 + values * (1.0 - sigma))


def weight_grad(inputs, deltas):
    channels = inputs.shape[-1]
    box_side = inputs.shape[1]
    padded = jnp.pad(inputs, ((0, 0), (1, 1), (1, 1), (0, 0)))
    flat_delta = deltas.reshape(-1, channels)
    blocks = []
    for shift_y in range(3):
        for shift_x in range(3):
            window = padded[
                :, shift_y : shift_y + box_side, shift_x : shift_x + box_side, :
            ].reshape(-1, channels)
            blocks.append(
                lax.dot_general(
                    window, flat_delta, (((0,), (0,)), ((), ())), preferred_element_type=jnp.float32
                )
            )
    return jnp.stack(blocks).reshape(3, 3, channels, channels)


def pick_rows(table, values):
    flat = values.reshape(values.shape[0], -1)
    return jnp.dot(table, flat, preferred_element_type=jnp.float32).astype(jnp.bfloat16)


def pick_back(table, values):
    return lax.dot_general(
        table, values, (((0,), (0,)), ((), ())), preferred_element_type=jnp.float32
    ).astype(jnp.bfloat16)


def body(in_map, tile_w, head_w1, head_w2, box_row, box_col, box_target, head_cot):
    tile_rows, tile_cols, channels = in_map.shape
    head_count = head_cot.shape[0]
    box_side = head_cot.shape[2]
    slot_count = box_target.shape[0]
    columns = lax.axis_size("col")
    capacity = slot_count // columns
    pair_count = columns * capacity
    padded = padded_2(in_map, (("row", 0), ("col", 1)), 1)
    preact = conv_pad(padded[None], tile_w, 0)[0]
    target = box_target[:, 0]
    occupied = target >= 0
    dest_col = jnp.where(occupied, target // head_count, 0)
    head_slot = jnp.where(occupied, target % head_count, 0)
    slot_ids = jnp.arange(slot_count, dtype=jnp.int32)
    same_dest = (dest_col[:, None] == dest_col[None, :]) & occupied[None, :]
    placing = jnp.sum(same_dest & (slot_ids[None, :] < slot_ids[:, None]), axis=1)
    pair_slot = dest_col * capacity + placing
    pair_ids = jnp.arange(pair_count, dtype=jnp.int32)
    send_map = ((pair_slot[None, :] == pair_ids[:, None]) & occupied[None, :]).astype(jnp.bfloat16)
    head_ids = jnp.arange(head_count, dtype=jnp.int32)
    head_hot = ((head_slot[:, None] == head_ids[None, :]) & occupied[:, None]).astype(jnp.bfloat16)
    pair_head = (
        jnp.dot(send_map, head_hot, preferred_element_type=jnp.float32)
        .astype(jnp.bfloat16)
        .reshape(columns, capacity, head_count)
    )
    top_row = box_row[:, 0]
    left_col = box_col[:, 0]
    zero_index = jnp.zeros((), jnp.int32)
    feature = jax.nn.silu(preact).astype(jnp.bfloat16)
    crops = jax.vmap(
        lambda y, x: lax.dynamic_slice(feature, (y, x, zero_index), (box_side, box_side, channels))
    )(top_row, left_col)
    outgoing = pick_rows(send_map, crops).reshape(columns, capacity, box_side, box_side, channels)
    arrived, arrived_head = (
        lax.all_to_all(outgoing, "col", split_axis=0, concat_axis=0, tiled=True),
        lax.all_to_all(pair_head, "col", split_axis=0, concat_axis=0, tiled=True),
    )
    arrived_head = arrived_head.reshape(pair_count, head_count)
    box_input = pick_back(arrived_head, arrived.reshape(pair_count, -1)).reshape(
        head_count, box_side, box_side, channels
    )
    factor = 1.0 / math.sqrt(lax.axis_size("row") * columns * head_count * box_side * box_side)
    cotangent = head_cot[:, 0]
    pre_one = conv_pad(box_input, head_w1, 1)
    hidden = jax.nn.silu(pre_one).astype(jnp.bfloat16)
    pre_two = conv_pad(hidden, head_w2, 1)
    delta_two = (cotangent.astype(jnp.float32) * silu_slope(pre_two)).astype(jnp.bfloat16)
    second_local = weight_grad(hidden, delta_two)
    delta_one = (conv_pad(delta_two, flip_weights(head_w2), 1) * silu_slope(pre_one)).astype(
        jnp.bfloat16
    )
    box_grads = conv_pad(delta_one, flip_weights(head_w1), 1).astype(jnp.bfloat16)
    sent_back = pick_rows(arrived_head, box_grads).reshape(
        columns, capacity, box_side, box_side, channels
    )
    returned = lax.all_to_all(sent_back, "col", split_axis=0, concat_axis=0, tiled=True)
    slot_grads = pick_back(send_map, returned.reshape(pair_count, -1)).reshape(
        slot_count, box_side, box_side, channels
    )
    first_local = weight_grad(box_input, delta_one)
    first_sum, second_sum = lax.psum((first_local, second_local), ("row", "col"))

    def add_box(slot, running):
        current = lax.dynamic_slice(
            running, (top_row[slot], left_col[slot], zero_index), (box_side, box_side, channels)
        )
        return lax.dynamic_update_slice(
            running,
            current + slot_grads[slot].astype(jnp.float32),
            (top_row[slot], left_col[slot], zero_index),
        )

    box_total = lax.fori_loop(
        0, slot_count, add_box, jnp.zeros((tile_rows, tile_cols, channels), jnp.float32)
    )
    delta_map = (box_total * silu_slope(preact)).astype(jnp.bfloat16)
    delta_rim = padded_2(delta_map, (("row", 0), ("col", 1)), 1)
    grad_map = conv_pad(delta_rim[None], flip_weights(tile_w), 0)[0].astype(jnp.bfloat16)
    return (grad_map, first_sum * factor, second_sum * factor)


def solution(mesh):
    in_specs = (
        P("row", "col", None),
        P(),
        P(),
        P(),
        P("row", "col"),
        P("row", "col"),
        P("row", "col"),
        P("row", "col", None, None, None),
    )
    out_specs = (P("row", "col", None), P(), P())
    return jax.shard_map(body, mesh=mesh, in_specs=in_specs, out_specs=out_specs, check_vma=False)
```

profile of v0, /device:TPU:98, one launch (start us, length us, event | category | flops | bytes accessed | tf_op | source)
XLA Modules:
  0.0 488.1 jit_solution(9538092367469643481)
XLA Ops:
  8.0 4.3 collective-permute-start.1
  12.3 1.9 collective-permute-start
  17.8 1.7 collective-permute-done
  20.6 5.2 %collective-permute-start.2 = (bf16[18,1,256]{2,1,0:T(2,128)(2,1)S(1)}, bf16[18,1,256]{2,1,0:T(2,128)(2,1)S(1)}, u32[]{:S(2)}, u32[]{:S(2)}) collective-permute-start(bf16[18,1,256]{2,1,0:T(2,128)(2,1)S(1)} %get-tuple-element.157), channel_id=1, source_target_pairs={{0,1},{1,2},{2,3},{3,4},{4,5},{5,6},{6,7},{8,9},{9,10},{10,11},{11... | collective-permute-start | bytes 27656 | tf_op jit(solution)/shard_map/ppermute | solution.py:17
  25.7 1.9 collective-permute-start.3
  27.7 4.9 %collective-permute-done.3 = bf16[18,1,256]{2,1,0:T(2,128)(2,1)S(1)} collective-permute-done((bf16[18,1,256]{2,1,0:T(2,128)(2,1)S(1)}, bf16[18,1,256]{2,1,0:T(2,128)(2,1)S(1)}, u32[]{:S(2)}, u32[]{:S(2)}) %collective-permute-start.3) | collective-permute-done | bytes 9248 | tf_op jit(solution)/shard_map/ppermute | solution.py:18
  35.2 41.9 %while.15 = (s32[]{:T(128)}, bf16[16,32,256]{2,0,1:T(8,128)(2,1)S(1)}, s32[16,3]{0,1:T(4,128)S(1)}, bf16[16,14,14,256]{3,2,1,0:T(8,128)(2,1)}, s32[]{:T(128)}) while((s32[]{:T(128)}, bf16[16,32,256]{2,0,1:T(8,128)(2,1)S(1)}, s32[16,3]{0,1:T(4,128)S(1)}, bf16[16,14,14,256]{3,2,1,0:T(8,128)(2,1)}, s32[]{:T(128)}) %tuple.61), condition=%wide.while_cond, body=%wide.while_body.sunk | while | flops 2 | bytes 415869 | solution.py:105
  77.2 2.4 reshape.125
  79.6 1.7 convolution_convert_fusion.1
  81.3 2.6 reshape.126
  83.9 3.6 copy.100
  87.6 5.2 %all-to-all-start.1 = ((bf16[8,2,14,14,256]{4,1,3,2,0:T(2,128)(2,1)}), bf16[8,2,14,14,256]{4,1,3,2,0:T(2,128)(2,1)}, u32[]{:S(2)}, u32[]{:S(2)}) async-start(bf16[8,2,14,14,256]{4,1,3,2,0:T(2,128)(2,1)} %copy.100), calls=%async_computation.1 | async-start | bytes 3211264 | tf_op jit(solution)/shard_map/all_to_all | solution.py:109
  93.8 32.7 %all-to-all-done.1 = bf16[8,2,14,14,256]{4,1,3,2,0:T(2,128)(2,1)} async-done(((bf16[8,2,14,14,256]{4,1,3,2,0:T(2,128)(2,1)}), bf16[8,2,14,14,256]{4,1,3,2,0:T(2,128)(2,1)}, u32[]{:S(2)}, u32[]{:S(2)}) %all-to-all-start.1) | async-done | bytes 1605664 | tf_op jit(solution)/shard_map/all_to_all | solution.py:109
  126.4 6.7 %all-to-all-start = ((bf16[8,2,4]{2,1,0:T(2,128)(2,1)}), bf16[8,2,4]{2,1,0:T(2,128)(2,1)S(1)}, u32[]{:S(2)}, u32[]{:S(2)}) async-start(bf16[8,2,4]{2,1,0:T(2,128)(2,1)} %bitcast.9), calls=%async_computation | async-start | bytes 8192 | tf_op jit(solution)/shard_map/all_to_all | solution.py:110
  133.1 1.7 copy.101
  134.8 2.1 reshape.127
  137.5 1.8 convolution_convert_fusion.3
  150.5 1.3 fusion.8
  159.0 1.7 reshape.130
  160.7 3.7 copy.109
  164.4 6.9 %all-to-all-start.2 = ((bf16[8,2,14,14,256]{4,1,3,2,0:T(2,128)(2,1)}), bf16[8,2,14,14,256]{4,1,3,2,0:T(2,128)(2,1)S(1)}, u32[]{:S(2)}, u32[]{:S(2)}) async-start(bf16[8,2,14,14,256]{4,1,3,2,0:T(2,128)(2,1)} %copy.109), calls=%async_computation.2 | async-start | bytes 3211264 | tf_op jit(solution)/shard_map/all_to_all | solution.py:130
  189.3 15.8 %all-to-all-done.2 = bf16[8,2,14,14,256]{4,1,3,2,0:T(2,128)(2,1)S(1)} async-done(((bf16[8,2,14,14,256]{4,1,3,2,0:T(2,128)(2,1)}), bf16[8,2,14,14,256]{4,1,3,2,0:T(2,128)(2,1)S(1)}, u32[]{:S(2)}, u32[]{:S(2)}) %all-to-all-start.2) | async-done | bytes 1605664 | tf_op jit(solution)/shard_map/all_to_all | solution.py:130
  207.3 1.5 reshape.132
  208.9 90.9 %while.14 = (s32[]{:T(128)}, f32[16,32,256]{2,0,1:T(8,128)S(1)}, s32[16]{0:T(128)S(1)}, s32[16]{0:T(128)S(1)}, bf16[16,14,14,256]{3,2,1,0:T(8,128)(2,1)S(1)}, /*index=5*/s32[]{:T(128)}, s32[]{:T(128)}, s32[]{:T(128)}, s32[]{:T(128)}) while((s32[]{:T(128)}, f32[16,32,256]{2,0,1:T(8,128)S(1)}, s32[16]{0:T(128)S(1)}, s32[16]{0:T(128)S(1)}, ...), condition=%wide.region_2.3_spmd, body=%wide.region_1.2_spmd.sunk | while | flops 100360 | bytes 1706193 | solution.py:147
  300.1 1.9 collective-permute-start.4
  302.0 5.8 %collective-permute-start.5 = (bf16[1,32,256]{2,0,1:T(2,128)(2,1)S(1)}, bf16[1,32,256]{2,0,1:T(2,128)(2,1)S(1)}, u32[]{:S(2)}, u32[]{:S(2)}) collective-permute-start(bf16[1,32,256]{2,0,1:T(2,128)(2,1)S(1)} %get-tuple-element.160), channel_id=1, source_target_pairs={{8,0},{16,8},{24,16},{32,24},{40,32},{48,40},{56,48},{64,56},{72,6... | collective-permute-start | bytes 49160 | tf_op jit(solution)/shard_map/ppermute | solution.py:18
  307.8 155.4 %all-reduce.5.cloned.1.call-done = (f32[3,3,256,256]{3,2,1,0:T(8,128)}, f32[3,3,256,256]{3,2,1,0:T(8,128)}) async-done(((f32[3,3,256,256]{3,2,1,0:T(8,128)}, f32[3,3,256,256]{3,2,1,0:T(8,128)}), (f32[3,3,256,256]{3,2,1,0:T(8,128)}, f32[3,3,256,256]{3,2,1,0:T(8,128)})) %all-reduce.5.cloned.1.call-update) | async-done | bytes 4718608 | tf_op jit(solution)/shard_map/psum | solution.py:135
  463.2 3.4 broadcast_multiply_fusion.1
  466.7 5.5 %collective-permute-start.6 = (bf16[18,1,256]{2,0,1:T(8,128)(2,1)S(1)}, bf16[18,1,256]{2,0,1:T(8,128)(2,1)S(1)}, u32[]{:S(2)}, u32[]{:S(2)}) collective-permute-start(bf16[18,1,256]{2,0,1:T(8,128)(2,1)S(1)} %get-tuple-element.155), channel_id=1, source_target_pairs={{0,1},{1,2},{2,3},{3,4},{4,5},{5,6},{6,7},{8,9},{9,10},{10,11},{11... | collective-permute-start | bytes 27656 | tf_op jit(solution)/shard_map/ppermute | solution.py:17
  472.1 1.9 collective-permute-start.7
  474.1 1.6 broadcast_multiply_fusion
  475.7 3.2 collective-permute-done.7
  (311 shorter events, 120.0 us)
Async XLA Ops:
  7.2 137.5 %copy-start = (bf16[3,3,256,256]{3,2,1,0:T(8,128)(2,1)S(1)}, bf16[3,3,256,256]{3,2,1,0:T(8,128)(2,1)}, u32[]{:S(2)}) copy-start(bf16[3,3,256,256]{3,2,1,0:T(8,128)(2,1)} %param.13) | copy-start | bytes 3538948
  8.0 12.5 %collective-permute-start.1 = (bf16[1,32,256]{2,1,0:T(8,128)(2,1)S(1)}, bf16[1,32,256]{2,1,0:T(8,128)(2,1)S(1)}, u32[]{:S(2)}, u32[]{:S(2)}) collective-permute-start(bf16[1,32,256]{2,1,0:T(8,128)(2,1)S(1)} %get-tuple-element.161), channel_id=1, source_target_pairs={{8,0},{16,8},{24,16},{32,24},{40,32},{48,40},{56,48},{64,56},{72,6... | collective-permute-start | bytes 49160 | tf_op jit(solution)/shard_map/ppermute | solution.py:18
  12.3 7.2 %collective-permute-start = (bf16[1,32,256]{2,1,0:T(8,128)(2,1)S(1)}, bf16[1,32,256]{2,1,0:T(8,128)(2,1)S(1)}, u32[]{:S(2)}, u32[]{:S(2)}) collective-permute-start(bf16[1,32,256]{2,1,0:T(8,128)(2,1)S(1)} %get-tuple-element.162), channel_id=1, source_target_pairs={{0,8},{8,16},{16,24},{24,32},{32,40},{40,48},{48,56},{56,64},{64,7... | collective-permute-start | bytes 49160 | tf_op jit(solution)/shard_map/ppermute | solution.py:17
  20.5 12.6 %copy-start.22 = (bf16[3,3,256,256]{3,2,1,0:T(8,128)(2,1)S(1)}, bf16[3,3,256,256]{3,2,1,0:T(8,128)(2,1)}, u32[]{:S(2)}) copy-start(bf16[3,3,256,256]{3,2,1,0:T(8,128)(2,1)} %param.11) | copy-start | bytes 3538948
  20.5 12.6 %copy-start.25 = (pred[8,5]{0,1:T(8,128)(4,1)S(1)}, pred[8,5]{0,1:T(8,128)(4,1)}, u32[]{:S(2)}) copy-start(pred[8,5]{0,1:T(8,128)(4,1)} %constant.124) | copy-start | bytes 124
  20.6 7.1 %collective-permute-start.2 = (bf16[18,1,256]{2,1,0:T(2,128)(2,1)S(1)}, bf16[18,1,256]{2,1,0:T(2,128)(2,1)S(1)}, u32[]{:S(2)}, u32[]{:S(2)}) collective-permute-start(bf16[18,1,256]{2,1,0:T(2,128)(2,1)S(1)} %get-tuple-element.157), channel_id=1, source_target_pairs={{0,1},{1,2},{2,3},{3,4},{4,5},{5,6},{6,7},{8,9},{9,10},{10,11},{11... | collective-permute-start | bytes 27656 | tf_op jit(solution)/shard_map/ppermute | solution.py:17
  25.7 6.9 %collective-permute-start.3 = (bf16[18,1,256]{2,1,0:T(2,128)(2,1)S(1)}, bf16[18,1,256]{2,1,0:T(2,128)(2,1)S(1)}, u32[]{:S(2)}, u32[]{:S(2)}) collective-permute-start(bf16[18,1,256]{2,1,0:T(2,128)(2,1)S(1)} %get-tuple-element.158), channel_id=1, source_target_pairs={{1,0},{2,1},{3,2},{4,3},{5,4},{6,5},{7,6},{9,8},{10,9},{11,10},{12... | collective-permute-start | bytes 27656 | tf_op jit(solution)/shard_map/ppermute | solution.py:18
  87.6 5.2 %copy-start.24 = (s32[16,1]{0,1:T(1,128)S(1)}, s32[16,1]{0,1:T(1,128)}, u32[]{:S(2)}) copy-start(s32[16,1]{0,1:T(1,128)} %param.16) | copy-start | bytes 196
  87.6 38.8 %all-to-all-start.1 = ((bf16[8,2,14,14,256]{4,1,3,2,0:T(2,128)(2,1)}), bf16[8,2,14,14,256]{4,1,3,2,0:T(2,128)(2,1)}, u32[]{:S(2)}, u32[]{:S(2)}) async-start(bf16[8,2,14,14,256]{4,1,3,2,0:T(2,128)(2,1)} %copy.100), calls=%async_computation.1 | async-start | bytes 3211264 | tf_op jit(solution)/shard_map/all_to_all | solution.py:109
  126.4 11.1 %all-to-all-start = ((bf16[8,2,4]{2,1,0:T(2,128)(2,1)}), bf16[8,2,4]{2,1,0:T(2,128)(2,1)S(1)}, u32[]{:S(2)}, u32[]{:S(2)}) async-start(bf16[8,2,4]{2,1,0:T(2,128)(2,1)} %bitcast.9), calls=%async_computation | async-start | bytes 8192 | tf_op jit(solution)/shard_map/all_to_all | solution.py:110
  140.6 12.0 %copy-start.8 = (bf16[4,14,14,256]{3,2,1,0:T(8,128)(2,1)}, bf16[4,14,14,256]{3,2,1,0:T(8,128)(2,1)S(1)}, u32[]{:S(2)}) copy-start(bf16[4,14,14,256]{3,2,1,0:T(8,128)(2,1)S(1)} %reshape.128) | copy-start | bytes 1204228
  141.0 1.3 copy-start.20
  143.5 1.2 copy-start.13
  149.3 1.2 copy-start.14
  152.6 1.1 copy-start.6
  152.6 1.1 copy-start.12
  153.7 2.4 copy-start.21
  164.4 6.9 %copy-start.7 = (bf16[14,4,16,256]{3,2,1,0:T(8,128)(2,1)S(1)}, bf16[14,4,16,256]{3,2,1,0:T(8,128)(2,1)}, u32[]{:S(2)}) copy-start(bf16[14,4,16,256]{3,2,1,0:T(8,128)(2,1)} %copy-done.6) | copy-start | bytes 1376260
  164.4 6.9 %copy-start.9 = (bf16[4,14,14,256]{3,2,1,0:T(8,128)(2,1)S(1)}, bf16[4,14,14,256]{3,2,1,0:T(8,128)(2,1)}, u32[]{:S(2)}) copy-start(bf16[4,14,14,256]{3,2,1,0:T(8,128)(2,1)} %copy-done.8) | copy-start | bytes 1204228
  164.4 40.7 %all-to-all-start.2 = ((bf16[8,2,14,14,256]{4,1,3,2,0:T(2,128)(2,1)}), bf16[8,2,14,14,256]{4,1,3,2,0:T(2,128)(2,1)S(1)}, u32[]{:S(2)}, u32[]{:S(2)}) async-start(bf16[8,2,14,14,256]{4,1,3,2,0:T(2,128)(2,1)} %copy.109), calls=%async_computation.2 | async-start | bytes 3211264 | tf_op jit(solution)/shard_map/all_to_all | solution.py:130
  171.3 291.9 %all-reduce.5.cloned.1.call-start = ((), (), s32[]{:S(2)}) async-start(), calls=%async_computation.3 | async-start | bytes 9437184 | tf_op jit(solution)/shard_map/psum | solution.py:135
  178.7 1.2 copy-start.11
  207.3 1.6 copy-start.18
  207.3 1.6 copy-start.19
  208.9 90.9 %copy-start.3 = (f32[16,8,5,256]{3,0,2,1:T(8,128)S(1)}, f32[16,8,5,256]{3,0,2,1:T(8,128)}, u32[]{:S(2)}) copy-start(f32[16,8,5,256]{3,0,2,1:T(8,128)} %copy-done.2) | copy-start | bytes 1966084
  300.1 166.5 %collective-permute-start.4 = (bf16[1,32,256]{2,0,1:T(2,128)(2,1)S(1)}, bf16[1,32,256]{2,0,1:T(2,128)(2,1)S(1)}, u32[]{:S(2)}, u32[]{:S(2)}) collective-permute-start(bf16[1,32,256]{2,0,1:T(2,128)(2,1)S(1)} %get-tuple-element.159), channel_id=1, source_target_pairs={{0,8},{8,16},{16,24},{24,32},{32,40},{40,48},{48,56},{56,64},{64,7... | collective-permute-start | bytes 49160 | tf_op jit(solution)/shard_map/ppermute | solution.py:17
  302.0 164.6 %collective-permute-start.5 = (bf16[1,32,256]{2,0,1:T(2,128)(2,1)S(1)}, bf16[1,32,256]{2,0,1:T(2,128)(2,1)S(1)}, u32[]{:S(2)}, u32[]{:S(2)}) collective-permute-start(bf16[1,32,256]{2,0,1:T(2,128)(2,1)S(1)} %get-tuple-element.160), channel_id=1, source_target_pairs={{8,0},{16,8},{24,16},{32,24},{40,32},{48,40},{56,48},{64,56},{72,6... | collective-permute-start | bytes 49160 | tf_op jit(solution)/shard_map/ppermute | solution.py:18
  463.2 10.9 %copy-start.4 = (f32[3,3,256,256]{3,2,1,0:T(8,128)S(1)}, f32[3,3,256,256]{3,2,1,0:T(8,128)}, u32[]{:S(2)}) copy-start(f32[3,3,256,256]{3,2,1,0:T(8,128)} %get-tuple-element.146) | copy-start | bytes 7077892
  466.7 9.0 %collective-permute-start.6 = (bf16[18,1,256]{2,0,1:T(8,128)(2,1)S(1)}, bf16[18,1,256]{2,0,1:T(8,128)(2,1)S(1)}, u32[]{:S(2)}, u32[]{:S(2)}) collective-permute-start(bf16[18,1,256]{2,0,1:T(8,128)(2,1)S(1)} %get-tuple-element.155), channel_id=1, source_target_pairs={{0,1},{1,2},{2,3},{3,4},{4,5},{5,6},{6,7},{8,9},{9,10},{10,11},{11... | collective-permute-start | bytes 27656 | tf_op jit(solution)/shard_map/ppermute | solution.py:17
  472.1 6.8 %collective-permute-start.7 = (bf16[18,1,256]{2,0,1:T(8,128)(2,1)S(1)}, bf16[18,1,256]{2,0,1:T(8,128)(2,1)S(1)}, u32[]{:S(2)}, u32[]{:S(2)}) collective-permute-start(bf16[18,1,256]{2,0,1:T(8,128)(2,1)S(1)} %get-tuple-element.156), channel_id=1, source_target_pairs={{1,0},{2,1},{3,2},{4,3},{5,4},{6,5},{7,6},{9,8},{10,9},{11,10},{12... | collective-permute-start | bytes 27656 | tf_op jit(solution)/shard_map/ppermute | solution.py:18
  475.7 3.7 copy-start.23
  479.4 1.9 copy-start.1
  (6 other events, 5.5 us)
Sparse Core Ops, SparseCore 0:
  189.4 273.7 all-reduce.4
where the time goes:
time: 491 us; the launch traced here: 488 us
  waiting for transfers between devices  214 us (44%)
  local copies, waits for them, and re-layouts  104 us (21%)
  loops' own time  63.1 us (13%)
  starting transfers between devices  47.2 us (10%)
  matrix products  30.9 us (6%)
  between operations  14.8 us (3%)
  other arithmetic  13.8 us (3%)
    psum x1, waiting for transfers between devices, body(): lax.psum((first_local, second_local), ('row', 'col'))  155 us
    another operation x1, loops' own time, body(): lax.fori_loop(0, slot_count, add_box, jnp.zeros((tile_rows, tile_cols, ch...  62.9 us
    gather x64, local copies, waits for them, and re-layouts  41.8 us
    all_to_all x1, waiting for transfers between devices, body(): lax.all_to_all(outgoing, 'col', split_axis=0, concat_axis=0, tiled=True)  32.7 us
    dot_general x18, matrix products, weight_grad(): lax.dot_general(window, flat_delta, (((0,), (0,)), ((), ())), preferred_e...  18.9 us
    all_to_all x1, waiting for transfers between devices, body(): lax.all_to_all(sent_back, 'col', split_axis=0, concat_axis=0, tiled=True)  15.8 us
    ppermute x4, starting transfers between devices, padded_2(): before = lax.ppermute(last, axis, up)  14.5 us
    ppermute x4, starting transfers between devices, padded_2(): after = lax.ppermute(leading, axis, down)  13.9 us
  transfers between devices with their start and end apart: 12, of which 7 were waited for; matrix products, arithmetic and copies ran while one was open for 13% of the time, Pallas kernels for 0%

commit v1 on v0

--- a/solution.py
+++ b/solution.py
@@ -132,7 +132,7 @@
         slot_count, box_side, box_side, channels
     )
     first_local = weight_grad(box_input, delta_one)
-    first_sum, second_sum = lax.psum((first_local, second_local), ("row", "col"))
+    first_sum, second_sum = lax.psum(lax.psum((first_local, second_local), "col"), "row")
 
     def add_box(slot, running):
         current = lax.dynamic_slice(

time: 491 us -> 474 us (0.965)
  waiting for transfers between devices: 214 us -> 172 us
  other arithmetic: 13.8 us -> 27.3 us
  local copies, waits for them, and re-layouts: 104 us -> 117 us
    psum x1 -> x2, waiting for transfers between devices: 155 us -> 72.9 us  [the longest x1 72.9 us: body(): lax.psum((first_local, second_local), 'col')]
    all_to_all x1, waiting for transfers between devices: 15.8 us -> 54.2 us  [body(): lax.all_to_all(sent_back, 'col', split_axis=0, concat_axis=0, tiled=True)]
    add x16, other arithmetic: 2.09 us -> 16.5 us  [add_box(): current + slot_grads[slot].astype(jnp.float32)]
    unnamed x56 -> x64, local copies, waits for them, and re-layouts: 5.42 us -> 10.3 us
  transfers between devices with their start and end apart: 12 -> 13, of which waited for: 7 -> 8; matrix products, arithmetic and copies ran while one was open for 13% -> 16% of each run, Pallas kernels for 0% -> 0%
where the time goes in v1:
time: 474 us; the launch traced here: 470 us
  waiting for transfers between devices  172 us (36%)
  local copies, waits for them, and re-layouts  117 us (25%)
  loops' own time  63.1 us (13%)
  starting transfers between devices  46.3 us (10%)
  matrix products  29.9 us (6%)
  other arithmetic  27.3 us (6%)
  between operations  14.8 us (3%)
    psum x1, waiting for transfers between devices, body(): lax.psum((first_local, second_local), 'col')  72.9 us
    another operation x1, loops' own time, body(): lax.fori_loop(0, slot_count, add_box, jnp.zeros((tile_rows, tile_cols, ch...  62.9 us
    all_to_all x1, waiting for transfers between devices, body(): lax.all_to_all(sent_back, 'col', split_axis=0, concat_axis=0, tiled=True)  54.2 us
    gather x64, local copies, waits for them, and re-layouts  42.1 us
    all_to_all x1, waiting for transfers between devices, body(): lax.all_to_all(outgoing, 'col', split_axis=0, concat_axis=0, tiled=True)  32.5 us
    add x16, other arithmetic, add_box(): current + slot_grads[slot].astype(jnp.float32)  16.5 us
    ppermute x4, starting transfers between devices, padded_2(): after = lax.ppermute(leading, axis, down)  15.3 us
    dot_general x18, matrix products, weight_grad(): lax.dot_general(window, flat_delta, (((0,), (0,)), ((), ())), preferred_e...  15.2 us
  transfers between devices with their start and end apart: 13, of which 8 were waited for; matrix products, arithmetic and copies ran while one was open for 16% of the time, Pallas kernels for 0%

profile of v1, /device:TPU:98, one launch (start us, length us, event | category | flops | bytes accessed | tf_op | source)
XLA Modules:
  0.0 470.2 jit_solution(2804797186573654058)
XLA Ops:
  8.0 4.3 collective-permute-start.1
  12.3 1.9 collective-permute-start
  20.6 5.2 %collective-permute-start.2 = (bf16[18,1,256]{2,1,0:T(2,128)(2,1)S(1)}, bf16[18,1,256]{2,1,0:T(2,128)(2,1)S(1)}, u32[]{:S(2)}, u32[]{:S(2)}) collective-permute-start(bf16[18,1,256]{2,1,0:T(2,128)(2,1)S(1)} %get-tuple-element.159), channel_id=1, source_target_pairs={{0,1},{1,2},{2,3},{3,4},{4,5},{5,6},{6,7},{8,9},{9,10},{10,11},{11... | collective-permute-start | bytes 27656 | tf_op jit(solution)/shard_map/ppermute | solution.py:17
  25.7 1.9 collective-permute-start.3
  27.7 4.9 %collective-permute-done.3 = bf16[18,1,256]{2,1,0:T(2,128)(2,1)S(1)} collective-permute-done((bf16[18,1,256]{2,1,0:T(2,128)(2,1)S(1)}, bf16[18,1,256]{2,1,0:T(2,128)(2,1)S(1)}, u32[]{:S(2)}, u32[]{:S(2)}) %collective-permute-start.3) | collective-permute-done | bytes 9248 | tf_op jit(solution)/shard_map/ppermute | solution.py:18
  35.2 42.3 %while.15 = (s32[]{:T(128)}, bf16[16,32,256]{2,0,1:T(8,128)(2,1)S(1)}, s32[16,3]{0,1:T(4,128)S(1)}, bf16[16,14,14,256]{3,2,1,0:T(8,128)(2,1)}, s32[]{:T(128)}) while((s32[]{:T(128)}, bf16[16,32,256]{2,0,1:T(8,128)(2,1)S(1)}, s32[16,3]{0,1:T(4,128)S(1)}, bf16[16,14,14,256]{3,2,1,0:T(8,128)(2,1)}, s32[]{:T(128)}) %tuple.61), condition=%wide.while_cond, body=%wide.while_body.sunk | while | flops 2 | bytes 415869 | solution.py:105
  77.5 2.4 reshape.125
  81.7 2.6 reshape.126
  84.3 3.6 copy.100
  87.9 5.2 %all-to-all-start.1 = ((bf16[8,2,14,14,256]{4,1,3,2,0:T(2,128)(2,1)}), bf16[8,2,14,14,256]{4,1,3,2,0:T(2,128)(2,1)S(1)}, u32[]{:S(2)}, u32[]{:S(2)}) async-start(bf16[8,2,14,14,256]{4,1,3,2,0:T(2,128)(2,1)} %copy.100), calls=%async_computation.1 | async-start | bytes 3211264 | tf_op jit(solution)/shard_map/all_to_all | solution.py:109
  94.1 32.5 %all-to-all-done.1 = bf16[8,2,14,14,256]{4,1,3,2,0:T(2,128)(2,1)S(1)} async-done(((bf16[8,2,14,14,256]{4,1,3,2,0:T(2,128)(2,1)}), bf16[8,2,14,14,256]{4,1,3,2,0:T(2,128)(2,1)S(1)}, u32[]{:S(2)}, u32[]{:S(2)}) %all-to-all-start.1) | async-done | bytes 1605664 | tf_op jit(solution)/shard_map/all_to_all | solution.py:109
  126.7 6.7 %all-to-all-start = ((bf16[8,2,4]{2,1,0:T(2,128)(2,1)}), bf16[8,2,4]{2,1,0:T(2,128)(2,1)S(1)}, u32[]{:S(2)}, u32[]{:S(2)}) async-start(bf16[8,2,4]{2,1,0:T(2,128)(2,1)} %bitcast.9), calls=%async_computation | async-start | bytes 8192 | tf_op jit(solution)/shard_map/all_to_all | solution.py:110
  133.4 1.7 copy.101
  135.1 2.1 reshape.127
  137.7 1.8 convolution_convert_fusion.3
  158.0 1.9 reshape.134
  180.1 1.7 convolution_convert_fusion.2
  181.8 2.6 reshape.130
  184.5 3.7 copy.109
  188.2 7.4 %all-to-all-start.2 = ((bf16[8,2,14,14,256]{4,1,3,2,0:T(2,128)(2,1)}), bf16[8,2,14,14,256]{4,1,3,2,0:T(2,128)(2,1)}, u32[]{:S(2)}, u32[]{:S(2)}) async-start(bf16[8,2,14,14,256]{4,1,3,2,0:T(2,128)(2,1)} %copy.109), calls=%async_computation.2 | async-start | bytes 3211264 | tf_op jit(solution)/shard_map/all_to_all | solution.py:130
  195.6 54.2 %all-to-all-done.2 = bf16[8,2,14,14,256]{4,1,3,2,0:T(2,128)(2,1)} async-done(((bf16[8,2,14,14,256]{4,1,3,2,0:T(2,128)(2,1)}), bf16[8,2,14,14,256]{4,1,3,2,0:T(2,128)(2,1)}, u32[]{:S(2)}, u32[]{:S(2)}) %all-to-all-start.2) | async-done | bytes 1605664 | tf_op jit(solution)/shard_map/all_to_all | solution.py:130
  251.5 2.1 reshape.131
  253.6 2.1 convolution_convert_fusion
  255.7 2.4 reshape.132
  258.1 72.9 %all-reduce.9.cloned.1.call-done = (f32[3,3,256,256]{3,2,1,0:T(8,128)}, f32[3,3,256,256]{3,2,1,0:T(8,128)}) async-done(((f32[3,3,256,256]{3,2,1,0:T(8,128)}, f32[3,3,256,256]{3,2,1,0:T(8,128)}), (f32[3,3,256,256]{3,2,1,0:T(8,128)}, f32[3,3,256,256]{3,2,1,0:T(8,128)})) %all-reduce.9.cloned.1.call-update) | async-done | bytes 4718608 | tf_op jit(solution)/shard_map/psum | solution.py:135
  331.7 105.3 %while.14 = (s32[]{:T(128)}, f32[16,32,256]{2,0,1:T(8,128)S(1)}, s32[16]{0:T(128)S(1)}, s32[16]{0:T(128)S(1)}, bf16[16,14,14,256]{3,2,1,0:T(8,128)(2,1)}, /*index=5*/s32[]{:T(128)}, s32[]{:T(128)}, s32[]{:T(128)}, s32[]{:T(128)}) while((s32[]{:T(128)}, f32[16,32,256]{2,0,1:T(8,128)S(1)}, s32[16]{0:T(128)S(1)}, s32[16]{0:T(128)S(1)}, ...), condition=%wide.region_2.3_spmd, body=%wide.region_1.2_spmd.sunk | while | flops 100360 | bytes 1706193 | solution.py:147
  437.3 2.1 collective-permute-start.4
  439.4 5.8 %collective-permute-start.5 = (bf16[1,32,256]{2,0,1:T(2,128)(2,1)S(1)}, bf16[1,32,256]{2,0,1:T(2,128)(2,1)S(1)}, u32[]{:S(2)}, u32[]{:S(2)}) collective-permute-start(bf16[1,32,256]{2,0,1:T(2,128)(2,1)S(1)} %get-tuple-element.162), channel_id=1, source_target_pairs={{8,0},{16,8},{24,16},{32,24},{40,32},{48,40},{56,48},{64,56},{72,6... | collective-permute-start | bytes 49160 | tf_op jit(solution)/shard_map/ppermute | solution.py:18
  446.7 2.5 collective-permute-start.6
  449.2 3.3 collective-permute-start.7
  452.6 3.4 collective-permute-done.7
  458.3 3.4 broadcast_multiply_fusion.1
  (322 shorter events, 143.6 us)
Async XLA Ops:
  7.2 137.8 %copy-start = (bf16[3,3,256,256]{3,2,1,0:T(8,128)(2,1)S(1)}, bf16[3,3,256,256]{3,2,1,0:T(8,128)(2,1)}, u32[]{:S(2)}) copy-start(bf16[3,3,256,256]{3,2,1,0:T(8,128)(2,1)} %param.13) | copy-start | bytes 3538948
  8.0 12.5 %collective-permute-start.1 = (bf16[1,32,256]{2,1,0:T(8,128)(2,1)S(1)}, bf16[1,32,256]{2,1,0:T(8,128)(2,1)S(1)}, u32[]{:S(2)}, u32[]{:S(2)}) collective-permute-start(bf16[1,32,256]{2,1,0:T(8,128)(2,1)S(1)} %get-tuple-element.163), channel_id=1, source_target_pairs={{8,0},{16,8},{24,16},{32,24},{40,32},{48,40},{56,48},{64,56},{72,6... | collective-permute-start | bytes 49160 | tf_op jit(solution)/shard_map/ppermute | solution.py:18
  12.3 7.2 %collective-permute-start = (bf16[1,32,256]{2,1,0:T(8,128)(2,1)S(1)}, bf16[1,32,256]{2,1,0:T(8,128)(2,1)S(1)}, u32[]{:S(2)}, u32[]{:S(2)}) collective-permute-start(bf16[1,32,256]{2,1,0:T(8,128)(2,1)S(1)} %get-tuple-element.164), channel_id=1, source_target_pairs={{0,8},{8,16},{16,24},{24,32},{32,40},{40,48},{48,56},{56,64},{64,7... | collective-permute-start | bytes 49160 | tf_op jit(solution)/shard_map/ppermute | solution.py:17
  20.5 12.6 %copy-start.25 = (bf16[3,3,256,256]{3,2,1,0:T(8,128)(2,1)S(1)}, bf16[3,3,256,256]{3,2,1,0:T(8,128)(2,1)}, u32[]{:S(2)}) copy-start(bf16[3,3,256,256]{3,2,1,0:T(8,128)(2,1)} %param.11) | copy-start | bytes 3538948
  20.5 12.6 %copy-start.28 = (pred[8,5]{0,1:T(8,128)(4,1)S(1)}, pred[8,5]{0,1:T(8,128)(4,1)}, u32[]{:S(2)}) copy-start(pred[8,5]{0,1:T(8,128)(4,1)} %constant.124) | copy-start | bytes 124
  20.6 7.1 %collective-permute-start.2 = (bf16[18,1,256]{2,1,0:T(2,128)(2,1)S(1)}, bf16[18,1,256]{2,1,0:T(2,128)(2,1)S(1)}, u32[]{:S(2)}, u32[]{:S(2)}) collective-permute-start(bf16[18,1,256]{2,1,0:T(2,128)(2,1)S(1)} %get-tuple-element.159), channel_id=1, source_target_pairs={{0,1},{1,2},{2,3},{3,4},{4,5},{5,6},{6,7},{8,9},{9,10},{10,11},{11... | collective-permute-start | bytes 27656 | tf_op jit(solution)/shard_map/ppermute | solution.py:17
  25.7 6.9 %collective-permute-start.3 = (bf16[18,1,256]{2,1,0:T(2,128)(2,1)S(1)}, bf16[18,1,256]{2,1,0:T(2,128)(2,1)S(1)}, u32[]{:S(2)}, u32[]{:S(2)}) collective-permute-start(bf16[18,1,256]{2,1,0:T(2,128)(2,1)S(1)} %get-tuple-element.160), channel_id=1, source_target_pairs={{1,0},{2,1},{3,2},{4,3},{5,4},{6,5},{7,6},{9,8},{10,9},{11,10},{12... | collective-permute-start | bytes 27656 | tf_op jit(solution)/shard_map/ppermute | solution.py:18
  87.9 5.2 %copy-start.27 = (s32[16,1]{0,1:T(1,128)S(1)}, s32[16,1]{0,1:T(1,128)}, u32[]{:S(2)}) copy-start(s32[16,1]{0,1:T(1,128)} %param.16) | copy-start | bytes 196
  87.9 38.7 %all-to-all-start.1 = ((bf16[8,2,14,14,256]{4,1,3,2,0:T(2,128)(2,1)}), bf16[8,2,14,14,256]{4,1,3,2,0:T(2,128)(2,1)S(1)}, u32[]{:S(2)}, u32[]{:S(2)}) async-start(bf16[8,2,14,14,256]{4,1,3,2,0:T(2,128)(2,1)} %copy.100), calls=%async_computation.1 | async-start | bytes 3211264 | tf_op jit(solution)/shard_map/all_to_all | solution.py:109
  126.7 6.7 %copy-start.2 = (bf16[8,2,14,14,256]{4,1,3,2,0:T(2,128)(2,1)}, bf16[8,2,14,14,256]{4,1,3,2,0:T(2,128)(2,1)S(1)}, u32[]{:S(2)}) copy-start(bf16[8,2,14,14,256]{4,1,3,2,0:T(2,128)(2,1)S(1)} %all-to-all-done.1) | copy-start | bytes 4816900
  126.7 11.1 %all-to-all-start = ((bf16[8,2,4]{2,1,0:T(2,128)(2,1)}), bf16[8,2,4]{2,1,0:T(2,128)(2,1)S(1)}, u32[]{:S(2)}, u32[]{:S(2)}) async-start(bf16[8,2,4]{2,1,0:T(2,128)(2,1)} %bitcast.9), calls=%async_computation | async-start | bytes 8192 | tf_op jit(solution)/shard_map/all_to_all | solution.py:110
  133.4 197.7 %all-reduce.9.cloned.1.call-start = ((), (), s32[]{:S(2)}) async-start(), calls=%async_computation.4 | async-start | bytes 9437184 | tf_op jit(solution)/shard_map/psum | solution.py:135
  141.2 1.3 copy-start.23
  143.7 1.2 copy-start.14
  146.3 1.4 copy-start.17
  148.6 1.2 copy-start.15
  153.3 1.4 copy-start.13
  159.9 1.4 copy-start.10
  164.3 1.1 copy-start.16
  165.4 1.5 copy-start.6
  176.5 1.3 copy-start.24
  188.2 61.6 %all-to-all-start.2 = ((bf16[8,2,14,14,256]{4,1,3,2,0:T(2,128)(2,1)}), bf16[8,2,14,14,256]{4,1,3,2,0:T(2,128)(2,1)}, u32[]{:S(2)}, u32[]{:S(2)}) async-start(bf16[8,2,14,14,256]{4,1,3,2,0:T(2,128)(2,1)} %copy.109), calls=%async_computation.2 | async-start | bytes 3211264 | tf_op jit(solution)/shard_map/all_to_all | solution.py:130
  195.6 262.7 %all-reduce.7.cloned.1.call-start = ((), (), s32[]{:S(2)}) async-start(), calls=%async_computation.3 | async-start | bytes 9437184 | tf_op jit(solution)/shard_map/psum | solution.py:135
  331.7 105.3 %copy-start.4 = (f32[16,8,5,256]{3,0,2,1:T(8,128)S(1)}, f32[16,8,5,256]{3,0,2,1:T(8,128)}, u32[]{:S(2)}) copy-start(f32[16,8,5,256]{3,0,2,1:T(8,128)} %copy-done.3) | copy-start | bytes 1966084
  437.2 19.2 %copy-start.26 = (bf16[3,3,256,256]{3,2,1,0:T(8,128)(2,1)S(1)}, bf16[3,3,256,256]{3,2,1,0:T(8,128)(2,1)}, u32[]{:S(2)}) copy-start(bf16[3,3,256,256]{3,2,1,0:T(8,128)(2,1)} %param.11) | copy-start | bytes 3538948
  437.2 19.2 %copy-start.29 = (pred[8,5]{0,1:T(8,128)(4,1)S(1)}, pred[8,5]{0,1:T(8,128)(4,1)}, u32[]{:S(2)}) copy-start(pred[8,5]{0,1:T(8,128)(4,1)} %constant.124) | copy-start | bytes 124
  437.3 7.8 %collective-permute-start.4 = (bf16[1,32,256]{2,0,1:T(2,128)(2,1)S(1)}, bf16[1,32,256]{2,0,1:T(2,128)(2,1)S(1)}, u32[]{:S(2)}, u32[]{:S(2)}) collective-permute-start(bf16[1,32,256]{2,0,1:T(2,128)(2,1)S(1)} %get-tuple-element.161), channel_id=1, source_target_pairs={{0,8},{8,16},{16,24},{24,32},{32,40},{40,48},{48,56},{56,64},{64,7... | collective-permute-start | bytes 49160 | tf_op jit(solution)/shard_map/ppermute | solution.py:17
  439.4 7.3 %collective-permute-start.5 = (bf16[1,32,256]{2,0,1:T(2,128)(2,1)S(1)}, bf16[1,32,256]{2,0,1:T(2,128)(2,1)S(1)}, u32[]{:S(2)}, u32[]{:S(2)}) collective-permute-start(bf16[1,32,256]{2,0,1:T(2,128)(2,1)S(1)} %get-tuple-element.162), channel_id=1, source_target_pairs={{8,0},{16,8},{24,16},{32,24},{40,32},{48,40},{56,48},{64,56},{72,6... | collective-permute-start | bytes 49160 | tf_op jit(solution)/shard_map/ppermute | solution.py:18
  446.7 5.9 %collective-permute-start.6 = (bf16[18,1,256]{2,0,1:T(8,128)(2,1)S(1)}, bf16[18,1,256]{2,0,1:T(8,128)(2,1)S(1)}, u32[]{:S(2)}, u32[]{:S(2)}) collective-permute-start(bf16[18,1,256]{2,0,1:T(8,128)(2,1)S(1)} %get-tuple-element.157), channel_id=1, source_target_pairs={{0,1},{1,2},{2,3},{3,4},{4,5},{5,6},{6,7},{8,9},{9,10},{10,11},{11... | collective-permute-start | bytes 27656 | tf_op jit(solution)/shard_map/ppermute | solution.py:17
  449.2 6.8 %collective-permute-start.7 = (bf16[18,1,256]{2,0,1:T(8,128)(2,1)S(1)}, bf16[18,1,256]{2,0,1:T(8,128)(2,1)S(1)}, u32[]{:S(2)}, u32[]{:S(2)}) collective-permute-start(bf16[18,1,256]{2,0,1:T(8,128)(2,1)S(1)} %get-tuple-element.158), channel_id=1, source_target_pairs={{1,0},{2,1},{3,2},{4,3},{5,4},{6,5},{7,6},{9,8},{10,9},{11,10},{12... | collective-permute-start | bytes 27656 | tf_op jit(solution)/shard_map/ppermute | solution.py:18
  458.3 3.4 copy-start.5
  461.8 1.6 copy-start.1
  (11 other events, 9.4 us)
Sparse Core Ops, SparseCore 0:
  175.7 155.3 all-reduce.8
  334.5 121.5 all-reduce.6
